TPU v7x, 32 devices: a whole 2x2x4 slice. The times are simulated.
32 devices in a mesh: dp: 8 (over y, x, core), tensor: 4 (over z).
Axes of the slice: x: 2, y: 2, z: 4, core: 2. Of those that a mesh axis runs over, the one named last changes fastest.
Arguments:
- tokens: bfloat16 [16, 1024, 1152], P('dp', 'tensor'), may hold values from -6 to 6
- conditioning: float32 [16, 1152], P('dp'), may hold values from -12 to 12
- cotangent: bfloat16 [16, 1024, 1152], P('dp', 'tensor'), may hold values from -6 to 6
- query_weight: bfloat16 [1152, 1152], P('dp', 'tensor'), may hold values from -0.20623948 to 0.20623948
- key_weight: bfloat16 [1152, 1152], P('dp', 'tensor'), may hold values from -0.1875 to 0.1875
- value_weight: bfloat16 [1152, 1152], P('dp', 'tensor'), may hold values from -0.1875 to 0.1875
- out_weight: bfloat16 [1152, 1152], P('tensor', 'dp'), may hold values from -1 to 1
- up_weight: bfloat16 [1152, 4608], P('dp', 'tensor'), may hold values from -0.1875 to 0.1875
- down_weight: bfloat16 [4608, 1152], P('tensor', 'dp'), may hold values from -0.09375 to 0.09375
- ada_weight: bfloat16 [1152, 6912], P('dp', 'tensor'), may hold values from -0.109375 to 0.109375
- query_bias: float32 [1152], P('tensor'), may hold values from -3 to 3
- value_bias: float32 [1152], P('tensor'), may hold values from -3 to 3
- out_bias: float32 [1152], replicated, may hold values from -3 to 3
- up_bias: float32 [4608], P('tensor'), may hold values from -3 to 3
- down_bias: float32 [1152], replicated, may hold values from -3 to 3
- ada_bias: float32 [6912], P('tensor'), may hold values from -1.2 to 1.2
- threshold: float32 [1], replicated, may hold values from 0.5 to 1.5
Outputs:
- block_out: bfloat16 [16, 1024, 1152], P('dp', 'tensor')
- grad_tokens: float32 [16, 1024, 1152], P('dp', 'tensor')
- grad_conditioning: float32 [16, 1152], P('dp')
- grad_query_weight: float32 [1152, 1152], P('dp', 'tensor')
- grad_key_weight: float32 [1152, 1152], P('dp', 'tensor')
- grad_value_weight: float32 [1152, 1152], P('dp', 'tensor')
- grad_out_weight: float32 [1152, 1152], P('tensor', 'dp')
- grad_up_weight: float32 [1152, 4608], P('dp', 'tensor')
- grad_down_weight: float32 [4608, 1152], P('tensor', 'dp')
- grad_ada_weight: float32 [1152, 6912], P('dp', 'tensor')
- grad_query_bias: float32 [1152], P('tensor')
- grad_value_bias: float32 [1152], P('tensor')
- grad_out_bias: float32 [1152], replicated
- grad_up_bias: float32 [4608], P('tensor')
- grad_down_bias: float32 [1152], replicated
- grad_ada_bias: float32 [6912], P('tensor')
- query_clipped: bfloat16 [1152, 1152], P('dp', 'tensor')
- key_clipped: bfloat16 [1152, 1152], P('dp', 'tensor')
- query_bias_clipped: float32 [1152], P('tensor')
All inputs are finite; a program needn't handle non-finite values.
Results may differ from a plain program's by a relative error of at most 0.0131.
The roundings to bfloat16 on the way count: a program that leaves them out, or rounds other values in their place, can miss the bound.
Values may be sent and summed in bfloat16 or wider, within the bound.
A program may use at most 192 MiB of HBM per device.

v0:
```python
from functools import partial

import jax
import jax.numpy as jnp
from jax import lax
from jax.experimental import pallas as pl
from jax.experimental.pallas import tpu as pltpu
from jax.sharding import Mesh, PartitionSpec as P

HEAD_DIM=72
epsilon=1e-06
MESH = pl.DeviceIdType.MESH
AXES = ("y", "x", "core", "z")
ROWS, COLS, TOK = 144, 1152, 512
HS, KV0, KVW, AT0, ATW, ADA = 288, 256, 640, 768, 384, 1728
C = HEAD_DIM**-0.5
LOG2E = 1.4426950408889634
bf = jnp.bfloat16
f32 = jnp.float32
VM = pl.BlockSpec(memory_space=pltpu.VMEM)
HB = pl.BlockSpec(memory_space=pl.ANY)
S = jax.ShapeDtypeStruct
D = pltpu.SemaphoreType.DMA
V = pltpu.VMEM


def dg(a, b, ca, cb):
    return lax.dot_general(a, b, (((ca,), (cb,)), ((), ())), preferred_element_type=f32)


class Net:
    def __init__(self):
        self.y, self.x, self.c, self.z = (lax.axis_index(a) for a in AXES)
        y, x, c, z = self.y, self.x, self.c, self.z
        self.up, self.down = lax.rem(z + 1, 4), lax.rem(z + 3, 4)
        self.xn, self.yn, self.dn = (y, 1 - x, c, z), (1 - y, x, c, z), (1 - y, 1 - x, c, z)
        self.cn = (y, x, 1 - c, z)
        self.zpn, self.zmn = (y, x, c, self.up), (y, x, c, self.down)
        self.f, self.n = self.place(y, x)
        self.far = self.device(1 - self.f, self.n)
        self.near = self.device(self.f, 1 - self.n)

    def place(self, a, b):
        return (1 - self.c) * a + self.c * b, (1 - self.c) * b + self.c * a

    def device(self, f, n):
        y, x = self.place(f, n)
        return (y, x, self.c, self.z)

    def along_z(self, step):
        return (self.y, self.x, self.c, lax.rem(self.z + step, 4))

    def greet(self):
        bar = pltpu.get_barrier_semaphore()
        others = [self.xn, self.yn, self.dn]
        for dc in range(2):
            for dz in range(4):
                if dc or dz:
                    others.append((self.y, self.x, lax.rem(self.c + dc, 2), lax.rem(self.z + dz, 4)))
        for o in others:
            pl.semaphore_signal(bar, inc=1, device_id=o, device_id_type=MESH)
        pl.semaphore_wait(bar, len(others))


def remote(src, dst, send, recv, device):
    return pltpu.make_async_remote_copy(
        src_ref=src, dst_ref=dst, send_sem=send, recv_sem=recv, device_id=device, device_id_type=MESH
    )


def landed(ref, sem):
    pltpu.make_async_copy(ref, ref, sem).wait()


def gelu_pair(u):
    k = 0.7978845608028654
    u2 = u * u
    t = jnp.tanh(k * u * (1.0 + 0.044715 * u2))
    h = 0.5 * (1.0 + t)
    return u * h, h + 0.5 * u * (1.0 - t * t) * (k * (1.0 + 3.0 * 0.044715 * u2))


class Gather:
    def __init__(self, net, g, shard, send, zsend, recv):
        self.net, self.g, self.shard, self.send, self.zsend, self.recv = net, g, shard, send, zsend, recv

    def slot(self, t, f, n, c, z):
        y, x = self.net.place(f, n)
        row = pl.multiple_of((4 * y + 2 * x + c) * ROWS, 16)
        return self.g.at[t, pl.ds(row, ROWS), pl.ds(pl.multiple_of(z * COLS, 128), COLS)]

    def sem(self, t, f, n, c, z):
        y, x = self.net.place(f, n)
        return self.recv.at[t, 4 * y + 2 * x + c, z]

    def put(self, u, k, device, f, n, z, own=False):
        t = lax.div(u, 4)
        s = self.slot(t, f, n, self.net.c, z)
        return remote(self.shard.at[t] if own else s, s, self.send.at[u, k], self.sem(t, f, n, self.net.c, z), device)

    def arrived(self, t, f, n, c, z):
        landed(self.slot(t, f, n, c, z), self.sem(t, f, n, c, z))

    def nth(self, k):
        z = self.net.z
        after = ((0, 1, 2, 3), (1, 0, 2, 3), (2, 3, 1, 0), (3, 2, 1, 0))
        return sum(
            jnp.where(jnp.logical_and(z == i, k == j), after[i][j], 0)
            for i in range(4) for j in range(4)
        )

    def onward(self, t, k, zz, act, own=False):
        net = self.net
        s = self.slot(t, net.f, net.n, net.c, zz)
        src = self.shard.at[t] if own else s
        sem = self.sem(t, net.f, net.n, net.c, zz)
        up = jnp.logical_and(zz <= net.z, net.z < 3)
        down = jnp.logical_and(zz >= net.z, net.z > 0)

        @pl.when(up)
        def _():
            act(remote(src, s, self.zsend.at[t, k, 0], sem, net.zpn))

        @pl.when(down)
        def _():
            act(remote(src, s, self.zsend.at[t, k, 1], sem, net.zmn))

    def copies(self, u, own=False):
        net = self.net
        zz = net.z if own else self.nth(lax.rem(u, 4))
        f, n = net.f, net.n
        return (
            [self.put(u, 0, net.near, f, n, zz, own), self.put(u, 1, net.far, f, n, zz, own), self.put(u, 2, net.cn, f, n, zz, own)],
            [self.put(u, 3, net.far, f, 1 - n, zz), self.put(u, 4, net.cn, f, 1 - n, zz), self.put(u, 5, net.cn, 1 - f, n, zz)],
            [self.put(u, 6, net.cn, 1 - f, 1 - n, zz)],
        )

    def line(self, u):
        t, k = lax.div(u, 4), lax.rem(u, 4)
        pl.when(k == 0)(lambda: self.onward(t, k, self.net.z, lambda cp: cp.start(), True))

        @pl.when(k > 0)
        def _():
            zz = self.nth(k)
            self.arrived(t, self.net.f, self.net.n, self.net.c, zz)
            self.onward(t, k, zz, lambda cp: cp.start())

    def tok(self, p):
        self.token_rows.piece(p)

    def cot(self, p):
        self.cot_rows.piece(p)

    def mid(self, u):
        pl.when(jnp.logical_and(self.net.z > 0, self.net.z < 3))(lambda: self.line(u))

    def end(self, u):
        pl.when(lax.rem(self.net.z, 3) == 0)(lambda: self.line(u))

    def spread(self, u):
        k = lax.rem(u, 4)

        @pl.when(k == 0)
        def _():
            for cp in self.copies(u, True)[0]:
                cp.start()

        @pl.when(k > 0)
        def _():
            for cp in self.copies(u)[0]:
                cp.start()

    def across(self, u):
        net, t = self.net, lax.div(u, 4)
        zz = self.nth(lax.rem(u, 4))
        a, b, d = self.copies(u)[1]
        self.arrived(t, net.f, 1 - net.n, net.c, zz)
        a.start()
        b.start()
        self.arrived(t, 1 - net.f, net.n, net.c, zz)
        d.start()

    def corner(self, u):
        net, t = self.net, lax.div(u, 4)
        self.arrived(t, 1 - net.f, 1 - net.n, net.c, self.nth(lax.rem(u, 4)))
        self.copies(u)[2][0].start()

    def do(self, *steps):
        for step, u in steps:
            step(self, u if step in (Gather.tok, Gather.cot) else jnp.int32(u))

    def at(self, point, table):
        for p, steps in enumerate(table):
            if steps:
                pl.when(point == p)(lambda: self.do(*steps))

    def from_mate(self, t):
        def one(i, _):
            self.arrived(t, lax.div(i, 8), lax.rem(lax.div(i, 4), 2), 1 - self.net.c, lax.rem(i, 4))
            return 0

        lax.fori_loop(0, 16, one, 0)

    def finish(self):
        def one(u, _):
            for group in self.copies(u):
                for cp in group:
                    cp.wait_send()
            t, k = lax.div(u, 4), lax.rem(u, 4)
            self.onward(t, k, self.nth(k), lambda cp: cp.wait_send())
            return 0

        lax.fori_loop(0, 12, one, 0)


def rows_out(net, i):
    dc, dz = lax.div(net.z, 2), 2 * net.c + i
    here = jnp.logical_and(dc == net.c, dz == net.z)
    return (net.y, net.x, dc, dz), pl.multiple_of(lax.rem(net.z, 2) * 256, 256), here


class Rows:
    def __init__(self, net, src, dst, send, recv):
        self.net, self.src, self.dst, self.send, self.recv = net, src, dst, send, recv

    def local(self):
        for i in range(2):
            _, row, here = rows_out(self.net, i)

            @pl.when(here)
            def _():
                self.dst[pl.ds(row, 256)] = self.src[i]

    def copy(self, i, first, count):
        device, row, here = rows_out(self.net, i)
        return remote(
            self.src.at[i, pl.ds(first, count)], self.dst.at[pl.ds(row + first, count)],
            self.send.at[i], self.recv.at[lax.rem(self.net.z, 2)], device,
        ), jnp.logical_not(here)

    def piece(self, p):
        cp, cond = self.copy(p % 2, p // 2 * 64, 64)
        pl.when(cond)(cp.start)

    def sent(self):
        for i in range(2):
            cp, cond = self.copy(i, 0, 256)
            pl.when(cond)(cp.wait_send)

    def arrivals(self):
        net = self.net
        for k in range(2):
            here = jnp.logical_and(lax.div(net.z, 2) == net.c, 2 * net.c + k == net.z)
            pl.when(jnp.logical_not(here))(lambda: landed(self.dst.at[pl.ds(k * 256, 256)], self.recv.at[k]))


def normalize(v):
    mean = jnp.mean(v, axis=-1, keepdims=True)
    centred = v - mean
    r = lax.rsqrt(jnp.mean(centred * centred, axis=-1, keepdims=True) + epsilon)
    return centred * r, r


def by_rows(step, body):
    def one(i, _):
        body(pl.ds(pl.multiple_of(i * step, step), step))
        return 0

    lax.fori_loop(0, TOK // step, one, 0)


TABLE = (
    ((Gather.across, 5),),
    ((Gather.end, 7), (Gather.spread, 7)),
    ((Gather.mid, 9), (Gather.mid, 10), (Gather.corner, 8)),
    ((Gather.across, 6), (Gather.end, 9), (Gather.spread, 9)),
    ((Gather.mid, 11), (Gather.corner, 5)),
    ((Gather.across, 7), (Gather.end, 10), (Gather.spread, 10), (Gather.cot, 0), (Gather.cot, 1)),
    ((Gather.end, 11), (Gather.spread, 11), (Gather.corner, 6), (Gather.cot, 2)),
    ((Gather.across, 9), (Gather.cot, 3)),
    ((Gather.across, 10), (Gather.cot, 4), (Gather.cot, 5)),
    ((Gather.cot, 6),),
    ((Gather.across, 11), (Gather.corner, 9), (Gather.cot, 7)),
    (),
    ((Gather.corner, 10),),
    (),
    ((Gather.corner, 11),),
)


def forward_kernel(
    shard, tokens, cotangent, lift_own, ada, ada_bias, z_bias, out_bias,
    g, tok, cot, lift_rows, vectors, biases, x_out, qkv_out, kvo_out, att_out, lse, peak, branch_out, nm_out, act_out, gd_out, d2,
    tok_v, cot_v, lift, part, part_in, four, four_in, zall, x_ref, w, qkv, kvo, att, branch, qh, kh, vh, oh, gbt, act_buf, gd_buf, dbuf,
    gsend, gzsend, grecv, lsem, rsend, rrecv, small_send, small_recv, wsem, ksend, krecv, osem, asem, gdsem, dsem,
):
    net = Net()
    y, x, c, z = net.y, net.x, net.c, net.z
    plane = 2 * y + x
    net.greet()
    flow = Gather(net, g, shard, gsend, gzsend, grecv)
    lift[plane, c] = lift_own[...]
    small = [remote(lift.at[plane, c], lift.at[plane, c], small_send.at[0], small_recv.at[0], net.cn)]
    small[0].start()
    token_rows = Rows(net, tokens, tok_v, rsend.at[0], rrecv.at[0])
    cot_rows = Rows(net, cotangent, cot_v, rsend.at[1], rrecv.at[1])
    flow.token_rows, flow.cot_rows = token_rows, cot_rows
    flow.do((Gather.line, 0))
    own = [pltpu.make_async_copy(shard.at[t], flow.slot(t, net.f, net.n, c, z), lsem.at[t]) for t in range(3)]
    for cp in own:
        cp.start()

    landed(lift.at[plane, 1 - c], small_recv.at[0])
    peers = ((net.xn, 2 * y + 1 - x), (net.yn, 2 - 2 * y + x), (net.dn, 3 - plane))
    for k, (dev, _) in enumerate(peers):
        cp = remote(lift.at[plane], lift.at[plane], small_send.at[1 + k], small_recv.at[1 + k], dev)
        cp.start()
        small.append(cp)
    flow.do((Gather.spread, 0), (Gather.spread, 4), (Gather.line, 1))
    for k, (_, p) in enumerate(peers):
        landed(lift.at[p], small_recv.at[1 + k])
    every = jnp.concatenate([lift[p, k, 0:2] for p in range(4) for k in range(2)], axis=0).astype(bf)
    batch = 4 * y + 2 * x + c
    pick = lax.broadcasted_iota(jnp.int32, (COLS, ROWS), 0) == lax.broadcasted_iota(jnp.int32, (COLS, ROWS), 1) + batch * ROWS
    rows = dg(every, jnp.where(pick, 1.0, 0.0).astype(bf), 1, 0)
    lift_rows[...] = rows
    partial = dg(rows.astype(bf), ada[...], 1, 0)
    part[...] = jnp.zeros_like(part)
    for p in range(4):
        part[p, 0:4] = partial[4 * p : 4 * p + 4]
    for k, (dev, p) in enumerate(peers):
        cp = remote(part.at[p], part_in.at[k], small_send.at[4 + k], small_recv.at[4 + k], dev)
        cp.start()
        small.append(cp)
    flow.do((Gather.spread, 1), (Gather.line, 2), (Gather.across, 0), (Gather.spread, 2), (Gather.line, 3), (Gather.spread, 3))
    for k in range(3):
        landed(part_in.at[k], small_recv.at[4 + k])
    four[...] = part[plane] + part_in[0] + part_in[1] + part_in[2]
    cp = remote(four, four_in, small_send.at[7], small_recv.at[7], net.cn)
    cp.start()
    small.append(cp)
    landed(four_in, small_recv.at[7])
    zall[z] = four[...] + four_in[...] + ada_bias[...]
    zall[z, 4:5] = z_bias[...]
    for k in range(3):
        cp = remote(zall.at[z], zall.at[z], small_send.at[8 + k], small_recv.at[8 + k], net.along_z(k + 1))
        cp.start()
        small.append(cp)
    flow.do(
        (Gather.across, 4), (Gather.tok, 0), (Gather.tok, 1), (Gather.across, 1), (Gather.tok, 2), (Gather.tok, 3), (Gather.across, 2), (Gather.tok, 4), (Gather.tok, 5),
        (Gather.across, 3), (Gather.spread, 8), (Gather.tok, 6), (Gather.tok, 7), (Gather.line, 4),
    )
    token_rows.local()
    cot_rows.local()
    for k in range(3):
        landed(zall.at[lax.rem(z + 3 - k, 4)], small_recv.at[8 + k])
    pieces = [zall[k, pl.ds(z, 1)] for k in range(4)]
    half = COLS // 2
    vectors[0:1] = pieces[0][:, :COLS]
    vectors[1:2] = jnp.concatenate([pieces[0][:, COLS:], pieces[1][:, :half]], axis=1)
    vectors[2:3] = pieces[1][:, half:]
    vectors[3:4] = pieces[2][:, :COLS]
    vectors[4:5] = jnp.concatenate([pieces[2][:, COLS:], pieces[3][:, :half]], axis=1)
    vectors[5:6] = pieces[3][:, half:]
    vectors[6:8] = jnp.zeros((2, COLS), f32)
    nothing = jnp.zeros((1, HS), f32)
    for k in range(4):
        b = zall[k, 4:5]
        biases[k, 0:1] = jnp.concatenate([b[:, :HS], nothing, b[:, HS : 2 * HS], nothing], axis=1)
        biases[k, 1:2] = b[:, 2 * HS :]

    flow.do((Gather.corner, 0), (Gather.corner, 4), (Gather.corner, 1), (Gather.corner, 2))
    token_rows.arrivals()

    def first_norm(r):
        n, _ = normalize(tok_v[r].astype(f32))
        x_ref[r] = (n * (1.0 + vectors[1:2]) + vectors[0:1]).astype(bf)

    by_rows(64, first_norm)
    outs = [pltpu.make_async_copy(x_ref, x_out, osem.at[1]), pltpu.make_async_copy(tok_v, tok, osem.at[0])]
    for cp in outs:
        cp.start()
    flow.do((Gather.line, 5), (Gather.spread, 5), (Gather.mid, 6), (Gather.corner, 3))
    flow.from_mate(0)

    def load_w(t, k):
        return pltpu.make_async_copy(g.at[t, :, pl.ds(k * COLS, COLS)], w.at[k], wsem.at[k])

    own[0].wait()
    for k in range(4):
        load_w(0, k).start()

    def kv(k):
        return remote(qkv.at[k, :, pl.ds(KV0, KVW)], kvo.at[k], ksend.at[k], krecv.at[k], net.cn)

    for k in range(4):
        load_w(0, k).wait()
        qkv[k] = (dg(x_ref[...], w[k], 1, 0) + biases[k, 0:1]).astype(bf)
        kv(k).start()
        flow.do(*((), ((Gather.end, 6), (Gather.spread, 6), (Gather.across, 8)), ((Gather.mid, 7), (Gather.line, 8)), ())[k])
    cp = pltpu.make_async_copy(qkv, qkv_out, osem.at[2])
    cp.start()
    outs.append(cp)
    branch[...] = jnp.broadcast_to(out_bias[...], (TOK, COLS))


    def chunk(k, _):
        flow.at(2 * k, TABLE)
        kv(k).wait_recv()
        for j in range(4):
            a = j * HEAD_DIM
            qh[j] = qkv[k, :, a : a + HEAD_DIM]
            kh[j, :TOK] = qkv[k, :, HS + a : HS + a + HEAD_DIM]
            vh[j, :TOK] = qkv[k, :, 2 * HS + a : 2 * HS + a + HEAD_DIM]
            kh[j, TOK:] = kvo[k, :, HS - KV0 + a : HS - KV0 + a + HEAD_DIM]
            vh[j, TOK:] = kvo[k, :, 2 * HS - KV0 + a : 2 * HS - KV0 + a + HEAD_DIM]

        def head(j, _):
            h = k * 4 + j
            s = dg(kh[j], qh[j], 1, 1)
            m = jnp.max(s, axis=0, keepdims=True)
            p = jnp.exp2((s - m) * (C * LOG2E))
            l = jnp.sum(p, axis=0, keepdims=True)
            o = dg(vh[j], p.astype(bf), 0, 0) / l
            oh[j] = o.T.astype(bf)
            lse[h] = m * (C * LOG2E) + jnp.log2(l)
            peak[h] = jnp.broadcast_to(jnp.max(m, axis=1, keepdims=True) * C, (1, 128))
            pl.when(j == 1)(lambda: flow.at(2 * k + 1, TABLE))
            return 0

        lax.fori_loop(0, 4, head, 0)
        att[k] = jnp.concatenate([jnp.zeros((TOK, ATW - HS), bf)] + [oh[j] for j in range(4)], axis=1)
        branch[...] += dg(att[k], w[k, :, AT0:], 1, 1)
        return 0

    lax.fori_loop(0, 4, chunk, 0)
    for src, dst, k in ((kvo, kvo_out, 3), (att, att_out, 4), (branch, branch_out, 5)):
        cp = pltpu.make_async_copy(src, dst, osem.at[k])
        cp.start()
        outs.append(cp)
    outs[0].wait()

    def second_norm(r):
        after = tok_v[r].astype(f32) + vectors[2:3] * branch[r]
        n, _ = normalize(after)
        x_ref[r] = (n * (1.0 + vectors[4:5]) + vectors[3:4]).astype(bf)

    by_rows(64, second_norm)
    cp = pltpu.make_async_copy(x_ref, nm_out, osem.at[6])
    cp.start()
    outs[0] = cp
    flow.do((Gather.corner, 7),)
    flow.from_mate(1)
    own[1].wait()
    for k in range(4):
        load_w(1, k).start()

    def slope_store(k):
        i = lax.rem(k, 2)
        return pltpu.make_async_copy(gd_buf.at[i], gd_out.at[k], gdsem.at[i])

    def hidden(k, _):
        i = lax.rem(k, 2)
        pltpu.make_async_copy(g.at[1, :, pl.ds(pl.multiple_of(k * COLS, 128), COLS)], w.at[k], wsem.at[k]).wait()
        pl.when(k >= 2)(lambda: slope_store(k - 2).wait())
        gd_buf[i] = dg(x_ref[...], w[k], 1, 0)

        def activate(r):
            a, d = gelu_pair(gd_buf[i, r] + biases[k, 1:2])
            act_buf[k, r] = a.astype(bf)
            gd_buf[i, r] = d

        by_rows(64, activate)
        slope_store(k).start()
        pltpu.make_async_copy(act_buf.at[k], act_out.at[k], asem.at[k]).start()
        flow.at(8 + k, TABLE)
        return 0

    lax.fori_loop(0, 4, hidden, 0)
    cot_rows.arrivals()
    cp = pltpu.make_async_copy(cot_v, cot, osem.at[1])
    cp.start()
    outs.append(cp)

    def gated(r):
        x_ref[r] = (vectors[5:6] * cot_v[r].astype(f32)).astype(bf)

    outs[0].wait()
    by_rows(64, gated)
    gbt[...] = x_ref[...].T

    def down_store(k):
        i = lax.rem(k, 2)
        return pltpu.make_async_copy(dbuf.at[i], d2.at[:, pl.ds(pl.multiple_of(k * COLS, 128), COLS)], dsem.at[i])

    def down(k, _):
        i = lax.rem(k, 2)
        pl.when(k >= 2)(lambda: down_store(k - 2).wait())
        dbuf[i] = dg(gbt[...], act_buf[k], 1, 0).astype(bf)
        down_store(k).start()
        flow.at(12 + k, TABLE)
        return 0

    lax.fori_loop(0, 4, down, 0)
    for k in (2, 3):
        slope_store(k).wait()
        down_store(k).wait()
    for k in range(4):
        pltpu.make_async_copy(act_buf.at[k], act_out.at[k], asem.at[k]).wait()
    flow.from_mate(2)
    flow.finish()
    for cp in outs[1:]:
        cp.wait()
    for k in range(4):
        kv(k).wait_send()
    for cp in small:
        cp.wait_send()
    own[2].wait()
    token_rows.sent()
    cot_rows.sent()


def forward(shard, tokens, cotangent, lift_own, ada, ada_bias, z_bias, out_bias):
    rows = S((TOK, COLS), bf)
    wide = S((TOK, COLS), f32)
    return pl.pallas_call(
        forward_kernel,
        name="forward",
        out_shape=(
            S((3, 8 * ROWS, 4 * COLS), bf), rows, rows, S((16, ROWS), f32), S((8, COLS), f32), S((4, 2, COLS), f32),
            rows, S((4, TOK, COLS), bf), S((4, TOK, KVW), bf), S((4, TOK, ATW), bf), S((16, 1, TOK), f32),
            S((16, 1, 128), f32), wide, rows, S((4, TOK, COLS), bf), S((4, TOK, COLS), f32), S((8 * ROWS, 4 * COLS), bf),
        ),
        in_specs=[VM] * 8,
        out_specs=(HB, HB, HB, VM, VM, VM, HB, HB, HB, HB, VM, VM, HB, HB, HB, HB, HB),
        scratch_shapes=[
            V((TOK, COLS), bf), V((TOK, COLS), bf), V((4, 2, 8, COLS), f32), V((4, 8, ADA), f32), V((3, 8, ADA), f32),
            V((8, ADA), f32), V((8, ADA), f32), V((4, 8, ADA), f32), V((TOK, COLS), bf), V((4, COLS, COLS), bf),
            V((4, TOK, COLS), bf), V((4, TOK, KVW), bf), V((4, TOK, ATW), bf), V((TOK, COLS), f32),
            V((4, TOK, HEAD_DIM), bf), V((4, 2 * TOK, HEAD_DIM), bf), V((4, 2 * TOK, HEAD_DIM), bf), V((4, TOK, HEAD_DIM), bf),
            V((COLS, TOK), bf), V((4, TOK, COLS), bf), V((2, TOK, COLS), f32), V((2, COLS, COLS), bf),
            D((12, 7)), D((3, 4, 2)), D((3, 8, 4)), D((3,)), D((2, 2)), D((2, 2)), D((11,)), D((11,)), D((4,)), D((4,)), D((4,)),
            D((7,)), D((4,)), D((2,)), D((2,)),
        ],
        compiler_params=pltpu.CompilerParams(collective_id=1, has_side_effects=True, vmem_limit_bytes=60 * 2**20),
    )(shard, tokens, cotangent, lift_own, ada, ada_bias, z_bias, out_bias)


LINE = (0, 3, 1, 2)


class Scatter:
    def __init__(self, net, source, out, stage, out_sem, rc, far_in, near_in, line_in, side_in, acc, ctmp, ftmp,
                 csend, crecv, own_sem, ctmp_sem, fsend, frecv, ftmp_sem, nsend, nrecv, lsend, lrecv, srecv):
        self.__dict__.update(locals())

    def block(self, v, yy, xx, c):
        row = pl.multiple_of((4 * yy + 2 * xx + c) * ROWS, 16)
        return self.source(v).at[pl.ds(row, ROWS), pl.ds(LINE[v % 4] * COLS, COLS)]

    def places(self):
        return [(yy, xx) for yy in range(2) for xx in range(2)]

    def to_mate(self, v, yy, xx):
        return remote(
            self.block(v, yy, xx, 1 - self.net.c), self.rc.at[v, yy, xx],
            self.csend.at[v, yy, xx], self.crecv.at[v, yy, xx], self.net.cn,
        )

    def begin(self, v):
        for yy, xx in self.places():
            self.to_mate(v, yy, xx).start()

    def to_far(self, v, n):
        yy, xx = self.net.place(1 - self.net.f, n)
        return remote(self.acc.at[v % 4, yy, xx], self.far_in.at[v, n], self.fsend.at[v, n], self.frecv.at[v, n], self.net.far)

    def to_near(self, v):
        yy, xx = self.net.place(self.net.f, 1 - self.net.n)
        return remote(self.acc.at[v % 4, yy, xx], self.near_in.at[v], self.nsend.at[v], self.nrecv.at[v], self.net.near)

    def own_loads(self, v):
        return [
            pltpu.make_async_copy(self.block(v, yy, xx, self.net.c), self.acc.at[v % 4, yy, xx], self.own_sem.at[yy, xx])
            for yy, xx in self.places()
        ]

    def mate_loads(self, v, f):
        for n in range(2):
            yy, xx = self.net.place(f, n)
            yield pltpu.make_async_copy(self.rc.at[v, yy, xx], self.ctmp.at[f, n], self.ctmp_sem.at[f, n])

    def add(self, a, b):
        def one(i, _):
            r = pl.ds(pl.multiple_of(i * 48, 16), 48)
            a[r] = a[r] + b[r]
            return 0

        lax.fori_loop(0, ROWS // 48, one, 0)

    def fetch(self, v):
        if v >= 4:
            for n in range(2):
                self.to_far(v - 4, n).wait_send()
            self.to_near(v - 4).wait_send()
        for cp in self.own_loads(v):
            cp.start()
        for yy, xx in self.places():
            landed(self.rc.at[v, yy, xx], self.crecv.at[v, yy, xx])
        for f in (1 - self.net.f, self.net.f):
            for cp in self.mate_loads(v, f):
                cp.start()

    def core(self, v):
        for cp in self.own_loads(v):
            cp.wait()
        for f in (1 - self.net.f, self.net.f):
            for n, cp in enumerate(self.mate_loads(v, f)):
                cp.wait()
                yy, xx = self.net.place(f, n)
                self.add(self.acc.at[v % 4, yy, xx], self.ctmp.at[f, n])
                if f is not self.net.f:
                    self.to_far(v, n).start()

    def far_loads(self, v):
        return [pltpu.make_async_copy(self.far_in.at[v, n], self.ftmp.at[n], self.ftmp_sem.at[n]) for n in range(2)]

    def bring(self, v):
        for n, cp in enumerate(self.far_loads(v)):
            landed(self.far_in.at[v, n], self.frecv.at[v, n])
            cp.start()

    def far(self, v):
        for cp in self.far_loads(v):
            cp.wait()
        for n in (1 - self.net.n, self.net.n):
            yy, xx = self.net.place(self.net.f, n)
            self.add(self.acc.at[v % 4, yy, xx], self.ftmp.at[n])
            if n is not self.net.n:
                self.to_near(v).start()

    def near(self, v):
        landed(self.near_in.at[v], self.nrecv.at[v])
        self.add(self.near_in.at[v], self.acc.at[v % 4, self.net.y, self.net.x])

    def hop(self, v, h, act):
        net, zz = self.net, LINE[v % 4]
        if h < zz:

            @pl.when(net.z == h)
            def _():
                act(v, h, remote(self.near_in.at[v], self.line_in.at[v], self.lsend.at[v], self.lrecv.at[v], net.zpn))

        if 3 - h > zz:

            @pl.when(net.z == 3 - h)
            def _():
                side = 3 - h - 1 == zz
                dst = self.side_in.at[v // 4] if side else self.line_in.at[v]
                sem = self.srecv.at[v // 4] if side else self.lrecv.at[v]
                act(v, h, remote(self.near_in.at[v], dst, self.lsend.at[v], sem, net.zmn))

    def pass_on(self, v, h, cp):
        if h:
            landed(self.line_in.at[v], self.lrecv.at[v])
            self.add(self.near_in.at[v], self.line_in.at[v])
        cp.start()

    def line0(self, v):
        self.hop(v, 0, self.pass_on)

    def line1(self, v):
        self.hop(v, 1, self.pass_on)

    def line2(self, v):
        self.hop(v, 2, self.pass_on)

    def keep(self, t):
        return pltpu.make_async_copy(self.stage, self.out.at[t], self.out_sem)

    def last(self, v):
        t, zz = 2 - v // 4, LINE[v % 4]

        @pl.when(self.net.z == zz)
        def _():
            if zz > 0:
                landed(self.line_in.at[v], self.lrecv.at[v])
            if zz < 3:
                landed(self.side_in.at[v // 4], self.srecv.at[v // 4])
            if t < 2:
                self.keep(t + 1).wait()

            def one(i, _):
                r = pl.ds(pl.multiple_of(i * 16, 16), 16)
                total = self.near_in[v, r].astype(f32)
                if zz > 0:
                    total = total + self.line_in[v, r].astype(f32)
                if zz < 3:
                    total = total + self.side_in[v // 4, r].astype(f32)
                self.stage[r] = total
                return 0

            lax.fori_loop(0, ROWS // 16, one, 0)
            self.keep(t).start()

    def rows(self, p):
        self.block_back.piece(p)

    def toks(self, p):
        self.token_back.piece(p)

    def do(self, *steps):
        for step, v in steps:
            step(self, v)

    def at(self, point, table, base=0):
        for p, steps in enumerate(table):
            if steps:
                pl.when(point == base + p)(lambda: self.do(*steps))

    def finish(self):
        self.keep(0).wait()
        for v in range(12):
            for yy, xx in self.places():
                self.to_mate(v, yy, xx).wait_send()
            if v >= 8:
                for n in range(2):
                    self.to_far(v, n).wait_send()
                self.to_near(v).wait_send()
            for h in range(3):
                self.hop(v, h, lambda v, h, cp: cp.wait_send())


HIDDEN = (
    ((Scatter.core, 2), (Scatter.fetch, 3)),
    ((Scatter.bring, 0), (Scatter.far, 0), (Scatter.core, 3)),
    ((Scatter.begin, 4),),
    ((Scatter.bring, 1), (Scatter.far, 1)),
    ((Scatter.begin, 5),),
    ((Scatter.near, 0), (Scatter.line0, 0), (Scatter.fetch, 4), (Scatter.bring, 2)),
    ((Scatter.core, 4), (Scatter.far, 2), (Scatter.begin, 6)),
    ((Scatter.near, 1), (Scatter.line0, 1), (Scatter.fetch, 5)),
)
HEADS = (
    ((Scatter.far, 4), (Scatter.core, 7), (Scatter.rows, 0)),
    ((Scatter.bring, 5), (Scatter.rows, 1)),
    ((Scatter.far, 5), (Scatter.rows, 2)),
    ((Scatter.rows, 3),),
    ((Scatter.near, 4), (Scatter.line0, 4), (Scatter.rows, 4)),
    ((Scatter.bring, 6), (Scatter.far, 6), (Scatter.rows, 5)),
    ((Scatter.begin, 8), (Scatter.near, 5), (Scatter.line0, 5), (Scatter.rows, 6)),
    ((Scatter.bring, 7), (Scatter.far, 7), (Scatter.fetch, 8), (Scatter.line1, 0), (Scatter.line1, 1), (Scatter.rows, 7)),
    ((Scatter.core, 8), (Scatter.line1, 2), (Scatter.line1, 3)),
    ((Scatter.near, 6), (Scatter.line0, 6), (Scatter.line1, 4)),
    ((Scatter.begin, 9), (Scatter.line2, 0), (Scatter.line2, 1)),
    ((Scatter.fetch, 9), (Scatter.line2, 2), (Scatter.line2, 3), (Scatter.line1, 5)),
    ((Scatter.core, 9), (Scatter.near, 7), (Scatter.line0, 7), (Scatter.line2, 4)),
    ((Scatter.bring, 8), (Scatter.far, 8), (Scatter.line1, 6)),
    ((Scatter.begin, 10), (Scatter.last, 0), (Scatter.last, 1), (Scatter.line2, 5)),
    ((Scatter.fetch, 10), (Scatter.last, 2), (Scatter.last, 3), (Scatter.line1, 7)),
)


class Back:
    def __init__(self, net, src, dst, send, recv):
        self.net, self.src, self.dst, self.send, self.recv = net, src, dst, send, recv

    def copy(self, k, first, count):
        net = self.net
        dc, dz = lax.div(net.z, 2), 2 * net.c + k
        here = jnp.logical_and(dc == net.c, dz == net.z)
        rows, image = self.src.at[pl.ds(k * 256 + first, count)], self.dst.at[lax.rem(net.z, 2), pl.ds(first, count)]
        sem = self.recv.at[lax.rem(net.z, 2)]
        return remote(rows, image, self.send.at[k], sem, (net.y, net.x, dc, dz)), pltpu.make_async_copy(rows, image, sem), here

    def piece(self, p):
        cp, local, here = self.copy(p % 2, p // 2 * 64, 64)
        pl.when(jnp.logical_not(here))(cp.start)
        pl.when(here)(local.start)

    def sent(self):
        for k in range(2):
            cp, _, here = self.copy(k, 0, 256)
            pl.when(jnp.logical_not(here))(cp.wait_send)

    def arrivals(self):
        for i in range(2):
            landed(self.dst.at[i], self.recv.at[i])


def column_sum(v):
    return jnp.sum(v.astype(f32), axis=0, keepdims=True)


def backward_kernel(
    g, tok_in, cot_in, x_in, nm_in, qkv_in, kvo_in, att_in, lse, peak, branch_in, act_in, gd_in, d2, vectors, lift_rows, ada, down_bias,
    sums, block_rows, token_rows, d, rc, far_in, ada_grad, ada_bias_grad, lifted, totals,
    tok, cot, branch, gn, br, gb, gub, xt, gt, w1, act, dbuf, near_in, line_in, side_in, acc, ctmp, ftmp, mate_in,
    stage, bias, bias_in, terms, terms_in, image, pgl, pgl_in, four,
    out_sem, csend, crecv, own_sem, ctmp_sem, fsend, frecv, ftmp_sem, nsend, nrecv, lsend, lrecv, srecv,
    bsend, brecv, isem, w1_sem, w2_sem, act_sem, gd_sem, dsem, msend, mrecv, kvsem, small_send, small_recv,
):
    net = Net()
    y, x, c, z = net.y, net.x, net.c, net.z
    plane = 2 * y + x

    def fetch(src, dst, k):
        cp = pltpu.make_async_copy(src, dst, isem.at[k])
        cp.start()
        return cp

    first = [fetch(cot_in, cot, 0), fetch(nm_in, gub, 1), fetch(tok_in, tok, 2), fetch(branch_in, branch, 3)]

    def cols(ref, k):
        return ref.at[:, pl.ds(pl.multiple_of(zs(k) * COLS, 128), COLS)]

    def zs(k):
        return jnp.where(k == 0, 0, jnp.where(k == 1, 3, k - 1))

    def load_first(t, k):
        return pltpu.make_async_copy(cols(g.at[t], k), w1.at[lax.rem(k, 2)], w1_sem.at[lax.rem(k, 2)])

    def d_store(t, k):
        return pltpu.make_async_copy(dbuf, cols(d.at[t], k), dsem)

    load_first(1, jnp.int32(0)).start()
    net.greet()
    flow = Scatter(
        net, lambda v: d2 if v < 4 else d.at[2 - v // 4], sums, stage, out_sem, rc, far_in, near_in, line_in, side_in, acc, ctmp, ftmp,
        csend, crecv, own_sem, ctmp_sem, fsend, frecv, ftmp_sem, nsend, nrecv, lsend, lrecv, srecv,
    )
    for v in range(4):
        flow.begin(v)
    shift_attn, scale_attn, gate_attn, shift_mlp, scale_mlp, gate_mlp = [vectors[i : i + 1] for i in range(6)]
    terms[...] = jnp.zeros_like(terms)
    bias[...] = jnp.zeros_like(bias)
    for h in range(16):
        bias[h : h + 1, COLS:] = peak[h]
    gn[...] = jnp.zeros_like(gn)
    br[...] = jnp.zeros_like(br)
    first[0].wait()

    def gated(r):
        gb[r] = (gate_mlp * cot[r].astype(f32)).astype(bf)

    by_rows(64, gated)
    first[1].wait()
    xt[...] = gub[...].T

    def mlp(w2, gd):
        def loads(k):
            i = lax.rem(k, 2)
            return (
                load_first(1, k),
                pltpu.make_async_copy(cols(g.at[2], k), w2.at[i], w2_sem.at[i]),
                pltpu.make_async_copy(act_in.at[zs(k)], act.at[i], act_sem.at[i]),
                pltpu.make_async_copy(gd_in.at[zs(k)], gd.at[i], gd_sem.at[i]),
            )

        for cp in loads(jnp.int32(0))[1:]:
            cp.start()
        flow.do((Scatter.fetch, 0), (Scatter.core, 0), (Scatter.fetch, 1), (Scatter.core, 1), (Scatter.fetch, 2))

        def hidden(k, _):
            i = lax.rem(k, 2)
            for cp in loads(k):
                cp.wait()

            @pl.when(k < 3)
            def _():
                for cp in loads(k + 1):
                    cp.start()

            gub[...] = (dg(gb[...], w2[i], 1, 0) * gd[i]).astype(bf)
            bias[pl.ds(4 + zs(k), 1), :COLS] = column_sum(gub[...])
            br[...] += dg(act[i], w2[i], 1, 1)
            pl.when(k > 0)(lambda: d_store(1, k - 1).wait())
            flow.at(2 * k, HIDDEN)
            dbuf[...] = dg(xt[...], gub[...], 1, 0).astype(bf)
            d_store(1, k).start()
            gn[...] += dg(gub[...], w1[i], 1, 1)
            flow.at(2 * k + 1, HIDDEN)
            return 0

        lax.fori_loop(0, 4, hidden, 0)

    pl.run_scoped(mlp, V((2, COLS, COLS), bf), V((2, TOK, COLS), f32))
    load_first(0, jnp.int32(0)).start()
    d_store(1, jnp.int32(3)).wait()
    flow.do((Scatter.begin, 7), (Scatter.core, 5), (Scatter.bring, 3), (Scatter.far, 3))
    first[2].wait()
    first[3].wait()

    def second_norm(r):
        after = tok[r].astype(f32) + gate_attn * branch[r]
        n, s = normalize(after)
        mlp_out = br[r] + down_bias[...]
        gub[r] = (after + gate_mlp * mlp_out).astype(bf)
        go = cot[r].astype(f32)
        terms[5:6] += column_sum(go * mlp_out)
        gr = gn[r]
        terms[3:4] += column_sum(gr)
        terms[4:5] += column_sum(gr * n)
        e = gr * (1.0 + scale_mlp)
        ga = go + s * (e - jnp.mean(e, axis=-1, keepdims=True) - n * jnp.mean(e * n, axis=-1, keepdims=True))
        br[r] = ga
        terms[2:3] += column_sum(ga * branch[r])
        bias[9:10, :COLS] += column_sum(gb[r])
        low = (gate_attn * ga).astype(bf)
        bias[8:9, :COLS] += column_sum(low)
        gb[r] = low

    by_rows(64, second_norm)
    block_back = Back(net, gub, block_rows, bsend.at[0], brecv.at[0])
    flow.do((Scatter.near, 2), (Scatter.line0, 2), (Scatter.fetch, 6))
    flow.block_back = block_back
    flow.do((Scatter.core, 6),)
    load = fetch(x_in, cot, 0)
    gt[...] = gb[...].T
    flow.do((Scatter.near, 3), (Scatter.line0, 3), (Scatter.fetch, 7), (Scatter.bring, 4))
    gn[...] = jnp.zeros_like(gn)
    load.wait()
    xt[...] = cot[...].T

    def attention(kvo, att, qh, kh, vh, gh, dqh, dkh, dvh, dkm, dvm, mate_out):
        pack = cot

        def loads(k):
            i = lax.rem(k, 2)
            return (
                load_first(0, k),
                pltpu.make_async_copy(qkv_in.at[zs(k)], act.at[i], act_sem.at[i]),
                pltpu.make_async_copy(kvo_in.at[zs(k)], kvo, kvsem.at[0, i]),
                pltpu.make_async_copy(att_in.at[zs(k)], att.at[i], kvsem.at[1, i]),
            )

        for cp in loads(jnp.int32(0))[1:]:
            cp.start()

        def to_mate(k):
            return remote(mate_out, mate_in.at[lax.rem(k, 2)], msend, mrecv.at[k], net.cn)

        def complete(k):
            i = lax.rem(k, 2)
            to_mate(k).wait_send()
            landed(mate_in.at[i], mrecv.at[k])
            both = (branch[:, : 2 * HS] + mate_in[i, :, : 2 * HS].astype(f32)).astype(bf)
            pack[:, HS:] = jnp.concatenate([both, jnp.zeros((TOK, HS), bf)], axis=1)
            bias[pl.ds(zs(k), 1), :COLS] = column_sum(pack[...])
            gn[...] += dg(pack[...], w1[i], 1, 1)
            d1 = dg(xt[...], pack[:, :896], 1, 0)
            d2_ = dg(gt[...], att[i], 1, 0)
            dbuf[:, :AT0] = d1[:, :AT0].astype(bf)
            dbuf[:, AT0:896] = (d1[:, AT0:] + d2_[:, :128]).astype(bf)
            dbuf[:, 896:] = d2_[:, 128:].astype(bf)
            d_store(0, k).start()

        def chunk(k, _):
            i = lax.rem(k, 2)
            for cp in loads(k):
                cp.wait()
            ga = dg(gb[...], w1[i, :, AT0:], 1, 0).astype(bf)
            for j in range(4):
                a = j * HEAD_DIM
                gh[j] = ga[:, ATW - HS + a : ATW - HS + a + HEAD_DIM]
                qh[j] = act[i, :, a : a + HEAD_DIM]
                kh[j, :TOK] = act[i, :, HS + a : HS + a + HEAD_DIM]
                vh[j, :TOK] = act[i, :, 2 * HS + a : 2 * HS + a + HEAD_DIM]
                kh[j, TOK:] = kvo[:, HS - KV0 + a : HS - KV0 + a + HEAD_DIM]
                vh[j, TOK:] = kvo[:, 2 * HS - KV0 + a : 2 * HS - KV0 + a + HEAD_DIM]

            def head(j, _):
                kk, q, gg = kh[j], qh[j], gh[j]
                p = jnp.exp2(dg(kk, q, 1, 1) * (C * LOG2E) - lse[zs(k) * 4 + j])
                t = p * dg(vh[j], gg, 1, 1)
                inner = jnp.sum(t, axis=0, keepdims=True)
                ds = (t - p * inner).astype(bf)
                dv = dg(p.astype(bf), gg, 1, 0)
                dvh[j], dvm[j] = dv[:TOK], dv[TOK:].astype(bf)
                dk = dg(ds, q, 1, 0) * C
                dkh[j], dkm[j] = dk[:TOK], dk[TOK:].astype(bf)
                dqh[j] = (dg(kk, ds, 0, 0) * C).T.astype(bf)
                pl.when(jnp.logical_and(j == 1, k > 0))(lambda: complete(k - 1))

                @pl.when(jnp.logical_and(j == 1, k < 3))
                def _():
                    for cp in loads(k + 1):
                        cp.start()

                pl.when(jnp.logical_and(j == 2, k > 0))(lambda: d_store(0, k - 1).wait())
                flow.at(4 * k + j, HEADS)
                return 0

            lax.fori_loop(0, 4, head, 0)
            mate_out[...] = jnp.concatenate(
                [dkm[j] for j in range(4)] + [dvm[j] for j in range(4)] + [jnp.zeros((TOK, KVW - 2 * HS), bf)], axis=1,
            )
            to_mate(k).start()
            branch[:, : 2 * HS] = jnp.concatenate([dkh[j] for j in range(4)] + [dvh[j] for j in range(4)], axis=1)
            pack[:, :HS] = jnp.concatenate([dqh[j] for j in range(4)], axis=1)
            return 0

        lax.fori_loop(0, 4, chunk, 0)
        flow.do((Scatter.core, 10), (Scatter.bring, 9))
        complete(jnp.int32(3))
        flow.do((Scatter.far, 9), (Scatter.near, 8), (Scatter.line0, 8), (Scatter.last, 4), (Scatter.line2, 6), (Scatter.line2, 7))

    T = (4, TOK, HEAD_DIM)
    T2 = (4, 2 * TOK, HEAD_DIM)
    pl.run_scoped(
        attention, V((TOK, KVW), bf), V((2, TOK, ATW), bf), V(T, bf), V(T2, bf), V(T2, bf), V(T, bf), V(T, bf), V(T, f32), V(T, f32),
        V(T, bf), V(T, bf), V((TOK, KVW), bf),
    )

    def first_norm(r):
        n, s = normalize(tok[r].astype(f32))
        gr = gn[r]
        terms[0:1] += column_sum(gr)
        terms[1:2] += column_sum(gr * n)
        e = gr * (1.0 + scale_attn)
        gr = s * (e - jnp.mean(e, axis=-1, keepdims=True) - n * jnp.mean(e * n, axis=-1, keepdims=True))
        tok[r] = (br[r] + gr).astype(bf)

    by_rows(64, first_norm)
    token_back = Back(net, tok, token_rows, bsend.at[1], brecv.at[1])
    flow.token_back = token_back

    small = []

    def exchange(k, src, dst, dev):
        cp = remote(src, dst, small_send.at[k], small_recv.at[k], dev)
        cp.start()
        small.append(cp)

    def combine(k):
        bias[:, :COLS] += bias_in[k, :, :COLS]
        bias[:, COLS:] = jnp.maximum(bias[:, COLS:], bias_in[k, :, COLS:])

    peers = ((net.xn, 2 * y + 1 - x), (net.yn, 2 - 2 * y + x), (net.dn, 3 - plane))
    exchange(0, terms, terms_in, net.cn)
    four[0] = bias[...]
    exchange(1, four.at[0], bias_in.at[0], net.cn)
    d_store(0, jnp.int32(3)).wait()
    flow.begin(11)
    landed(terms_in, small_recv.at[0])
    image[plane, z] = (terms[...] + terms_in[...]).astype(bf).astype(f32)
    for k in range(3):
        exchange(2 + k, image.at[plane, z], image.at[plane, z], net.along_z(k + 1))
    landed(bias_in.at[0], small_recv.at[1])
    combine(0)
    four[1] = bias[...]
    for k in range(3):
        exchange(5 + k, four.at[1], bias_in.at[1 + k], net.along_z(k + 1))
    flow.do((Scatter.fetch, 11), (Scatter.near, 9), (Scatter.line0, 9), (Scatter.core, 11), (Scatter.bring, 10), (Scatter.far, 10), (Scatter.toks, 0), (Scatter.toks, 1))
    for k in range(3):
        landed(image.at[plane, lax.rem(z + 3 - k, 4)], small_recv.at[2 + k])
    for k, (dev, _) in enumerate(peers):
        exchange(8 + k, image.at[plane], image.at[plane], dev)
    flow.do((Scatter.bring, 11), (Scatter.far, 11), (Scatter.near, 10), (Scatter.line0, 10), (Scatter.line1, 8), (Scatter.toks, 2))
    for k, (_, p) in enumerate(peers):
        landed(image.at[p], small_recv.at[8 + k])
    every = [jnp.concatenate([image[p, q, i : i + 1] for p in range(4) for q in range(4)], axis=0) for i in range(6)]
    half = COLS // 2
    options = (
        (every[0], every[1][:, :half]), (every[1][:, half:], every[2]),
        (every[3], every[4][:, :half]), (every[4][:, half:], every[5]),
    )
    grad = sum(jnp.where(z == k, jnp.concatenate(o, axis=1), 0.0) for k, o in enumerate(options))
    low = grad.astype(bf)
    pgl[0] = dg(low, ada[...], 1, 1)
    for k in range(3):
        exchange(14 + k, pgl.at[0], pgl_in.at[k], net.along_z(k + 1))
    flow.do((Scatter.toks, 3), (Scatter.near, 11), (Scatter.line0, 11), (Scatter.toks, 4))
    ada_bias_grad[...] = column_sum(grad)
    ada_grad[...] = dg(lift_rows[...].astype(bf), low, 0, 0)
    for k in range(3):
        landed(bias_in.at[1 + k], small_recv.at[5 + k])
        combine(1 + k)
    four[2] = bias[...]
    for k, (dev, _) in enumerate(peers):
        exchange(11 + k, four.at[2], bias_in.at[4 + k], dev)
    flow.do((Scatter.line1, 9), (Scatter.toks, 5), (Scatter.line2, 8), (Scatter.line1, 10), (Scatter.toks, 6))
    for k in range(3):
        landed(pgl_in.at[k], small_recv.at[14 + k])
    lifted[plane, c] = pgl[0] + pgl_in[0] + pgl_in[1] + pgl_in[2]
    exchange(17, lifted.at[plane, c], lifted.at[plane, c], net.cn)
    flow.do((Scatter.line1, 11), (Scatter.line2, 9), (Scatter.toks, 7))
    landed(lifted.at[plane, 1 - c], small_recv.at[17])
    for k, (dev, _) in enumerate(peers):
        exchange(18 + k, lifted.at[plane], lifted.at[plane], dev)
    for k in range(3):
        landed(bias_in.at[4 + k], small_recv.at[11 + k])
        combine(4 + k)
    totals[...] = bias[...]
    flow.do((Scatter.last, 5), (Scatter.last, 6), (Scatter.last, 7), (Scatter.last, 8), (Scatter.line2, 10), (Scatter.last, 9), (Scatter.line2, 11), (Scatter.last, 10), (Scatter.last, 11))
    for k, (_, p) in enumerate(peers):
        landed(lifted.at[p], small_recv.at[18 + k])
    block_back.arrivals()
    token_back.arrivals()
    flow.finish()
    for cp in small:
        cp.wait_send()
    block_back.sent()
    token_back.sent()


def backward(*args):
    B = (ROWS, COLS)
    wide, rows = (TOK, COLS), (2, 256, COLS)
    pair = D((2,))
    return pl.pallas_call(
        backward_kernel,
        name="backward",
        out_shape=(
            S((3,) + B, f32), S(rows, bf), S(rows, bf), S((2, 8 * ROWS, 4 * COLS), bf), S((12, 2, 2) + B, bf), S((12, 2) + B, bf),
            S((ROWS, ADA), f32), S((1, ADA), f32), S((4, 2, 16, ROWS), f32), S((16, COLS + 128), f32),
        ),
        in_specs=[HB] * 8 + [VM, VM] + [HB] * 4 + [VM] * 4,
        out_specs=(HB,) * 6 + (VM,) * 4,
        scratch_shapes=[
            V(wide, bf), V(wide, bf), V(wide, f32), V(wide, f32), V(wide, f32), V(wide, bf), V(wide, bf), V((COLS, TOK), bf), V((COLS, TOK), bf),
            V((2, COLS, COLS), bf), V((2, TOK, COLS), bf), V((COLS, COLS), bf),
            V((12,) + B, bf), V((12,) + B, bf), V((3,) + B, bf), V((4, 2, 2) + B, bf), V((2, 2) + B, bf), V((2,) + B, bf), V((2, TOK, KVW), bf),
            V(B, f32), V((16, COLS + 128), f32), V((7, 16, COLS + 128), f32), V((8, COLS), f32), V((8, COLS), f32), V((4, 4, 8, COLS), f32),
            V((1, 16, ROWS), f32), V((3, 16, ROWS), f32), V((3, 16, COLS + 128), f32),
            D, D((12, 2, 2)), D((12, 2, 2)), D((2, 2)), D((2, 2)), D((12, 2)), D((12, 2)), pair, D((12,)), D((12,)), D((12,)), D((12,)), D((3,)),
            D((2, 2)), D((2, 2)), D((4,)), pair, pair, pair, pair, D, D, D((4,)), D((2, 2)), D((21,)), D((21,)),
        ],
        compiler_params=pltpu.CompilerParams(collective_id=2, has_side_effects=True, vmem_limit_bytes=62 * 2**20),
    )(*args)


def modulate_images(values, shift, scale):
    average = jnp.mean(values, axis=-1, keepdims=True)
    centred = values - average
    spread = jnp.mean(centred * centred, axis=-1, keepdims=True)
    return centred * lax.rsqrt(spread + epsilon) * (1.0 + scale[:, None, :]) + shift[:, None, :]


def product(left, right):
    return jnp.dot(left, right, preferred_element_type=jnp.float32)


def inner_rows(left, right):
    return lax.dot_general(
        left, right, (((0,), (0,)), ((), ())), preferred_element_type=jnp.float32
    )


def against(left, right):
    return lax.dot_general(
        left, right, (((1,), (1,)), ((), ())), preferred_element_type=jnp.float32
    )


def spread_rows(values):
    return lax.all_gather(values, "tensor", axis=1, tiled=True)


def fold_rows(values):
    return lax.psum_scatter(values, "tensor", scatter_dimension=1, tiled=True)


def spread_grads(values):
    return lax.all_gather(values, "tensor", axis=1, tiled=True)


def fold_grads(values):
    return lax.psum_scatter(values, "tensor", scatter_dimension=1, tiled=True)


def local(
    tokens,
    conditioning,
    cotangent,
    query_weight,
    key_weight,
    value_weight,
    out_weight,
    up_weight,
    down_weight,
    ada_weight,
    query_bias,
    value_bias,
    out_bias,
    up_bias,
    down_bias,
    ada_bias,
    threshold,
):
    images = tokens.shape[0]
    model_width = tokens.shape[2]
    gathered = (
        lax.all_gather(query_weight, "dp", axis=0, tiled=True),
        lax.all_gather(key_weight, "dp", axis=0, tiled=True),
        lax.all_gather(value_weight, "dp", axis=0, tiled=True),
        lax.all_gather(out_weight, "dp", axis=1, tiled=True),
        lax.all_gather(up_weight, "dp", axis=0, tiled=True),
        lax.all_gather(down_weight, "dp", axis=1, tiled=True),
        lax.all_gather(ada_weight, "dp", axis=0, tiled=True),
    )
    full_query, full_key, full_value, full_out, full_up, full_down, full_ada = gathered
    lifted_low = jax.nn.silu(conditioning).astype(jnp.bfloat16)
    own_columns = product(lifted_low, full_ada) + ada_bias
    modulation = lax.all_gather(own_columns, "tensor", axis=1, tiled=True)
    pieces = [
        modulation[:, piece_index * model_width : (piece_index + 1) * model_width]
        for piece_index in range(6)
    ]
    shift_attn, scale_attn, gate_attn, shift_mlp, scale_mlp, gate_mlp = pieces
    inputs = tokens.astype(jnp.float32)
    normed_attn = spread_rows(modulate_images(inputs, shift_attn, scale_attn).astype(jnp.bfloat16))
    length = normed_attn.shape[1]
    row_count = images * length
    flat_attn = normed_attn.reshape(row_count, model_width)
    local_width = full_query.shape[1]
    heads_here = local_width // HEAD_DIM
    queries = (product(flat_attn, full_query) + query_bias).astype(jnp.bfloat16)
    key_rows = product(flat_attn, full_key).astype(jnp.bfloat16)
    value_rows = (product(flat_attn, full_value) + value_bias).astype(jnp.bfloat16)
    block_rows = min(512, length)
    head_scale = HEAD_DIM ** (-0.5)

    def by_head(matrix):
        return matrix.reshape(images, length, heads_here, HEAD_DIM)

    def attend_image(bundle):
        queries_img, keys_img, values_img = bundle
        outputs, totals, highest = ([], [], [])
        for offset in range(0, length, block_rows):
            logits = (
                jnp.einsum(
                    "qhe,khe->hqk",
                    queries_img[offset : offset + block_rows],
                    keys_img,
                    preferred_element_type=jnp.float32,
                )
                * head_scale
            )
            row_top = jnp.max(logits, axis=2, keepdims=True)
            raised = jnp.exp(logits - row_top)
            summed = jnp.sum(raised, axis=2, keepdims=True)
            shares = (raised / summed).astype(jnp.bfloat16)
            outputs.append(
                jnp.einsum(
                    "hqk,khe->qhe", shares, values_img, preferred_element_type=jnp.float32
                ).astype(jnp.bfloat16)
            )
            totals.append(row_top[:, :, 0] + jnp.log(summed[:, :, 0]))
            highest.append(jnp.max(row_top[:, :, 0], axis=1))
        return (
            jnp.concatenate(outputs, 0),
            jnp.concatenate(totals, 1),
            jnp.max(jnp.stack(highest), axis=0),
        )

    attended, log_totals, image_peaks = lax.map(
        attend_image, (by_head(queries), by_head(key_rows), by_head(value_rows))
    )
    flat_attended = attended.reshape(row_count, local_width)
    branch_attn = (
        fold_rows(product(flat_attended, full_out).reshape(images, length, model_width)) + out_bias
    )
    after_attn = inputs + gate_attn[:, None, :] * branch_attn
    normed_mlp = spread_rows(modulate_images(after_attn, shift_mlp, scale_mlp).astype(jnp.bfloat16))
    flat_mlp = normed_mlp.reshape(row_count, model_width)
    upward = product(flat_mlp, full_up) + up_bias
    active = jax.nn.gelu(upward, approximate=True).astype(jnp.bfloat16)
    branch_mlp = (
        fold_rows(product(active, full_down).reshape(images, length, model_width)) + down_bias
    )
    block_out = (after_attn + gate_mlp[:, None, :] * branch_mlp).astype(jnp.bfloat16)
    peaks = lax.pmax(jnp.max(image_peaks, axis=0), "dp")
    again = (
        lax.all_gather(query_weight, "dp", axis=0, tiled=True),
        lax.all_gather(key_weight, "dp", axis=0, tiled=True),
        lax.all_gather(value_weight, "dp", axis=0, tiled=True),
        lax.all_gather(out_weight, "dp", axis=1, tiled=True),
        lax.all_gather(up_weight, "dp", axis=0, tiled=True),
        lax.all_gather(down_weight, "dp", axis=1, tiled=True),
        lax.all_gather(ada_weight, "dp", axis=0, tiled=True),
    )
    back_query, back_key, back_value, back_out, back_up, back_down, back_ada = again
    grad_out = cotangent.astype(jnp.float32)
    grad_branch_mlp = (gate_mlp[:, None, :] * grad_out).astype(jnp.bfloat16)
    grad_gate_mlp = jnp.sum(grad_out * branch_mlp, axis=1)
    flat_grad_mlp = spread_grads(grad_branch_mlp).reshape(row_count, model_width)
    grad_down_bias = jnp.sum(flat_grad_mlp, axis=0, dtype=jnp.float32)
    grad_down_weight = inner_rows(active, flat_grad_mlp)
    grad_active = against(flat_grad_mlp, back_down)
    _, gelu_pull = jax.vjp(partial(jax.nn.gelu, approximate=True), upward)
    grad_upward = gelu_pull(grad_active)[0].astype(jnp.bfloat16)
    grad_up_bias = jnp.sum(grad_upward, axis=0, dtype=jnp.float32)
    grad_up_weight = inner_rows(flat_mlp, grad_upward)
    grad_normed_mlp = fold_grads(against(grad_upward, back_up).reshape(images, length, model_width))
    _, mlp_pull = jax.vjp(modulate_images, after_attn, shift_mlp, scale_mlp)
    grad_after, grad_shift_mlp, grad_scale_mlp = mlp_pull(grad_normed_mlp)
    grad_after = grad_out + grad_after
    grad_branch_attn = (gate_attn[:, None, :] * grad_after).astype(jnp.bfloat16)
    grad_gate_attn = jnp.sum(grad_after * branch_attn, axis=1)
    flat_grad_attn = spread_grads(grad_branch_attn).reshape(row_count, model_width)
    grad_out_bias = jnp.sum(flat_grad_attn, axis=0, dtype=jnp.float32)
    grad_out_weight = inner_rows(flat_attended, flat_grad_attn)
    grad_attended = against(flat_grad_attn, back_out).astype(jnp.bfloat16)

    def attend_back(bundle):
        queries_img, keys_img, values_img, grads_img, totals_img = bundle
        query_parts = []
        grad_keys_img = jnp.zeros(keys_img.shape, jnp.float32)
        grad_values_img = jnp.zeros(values_img.shape, jnp.float32)
        for offset in range(0, length, block_rows):
            query_block = queries_img[offset : offset + block_rows]
            grad_block = grads_img[offset : offset + block_rows]
            logits = (
                jnp.einsum(
                    "qhe,khe->hqk", query_block, keys_img, preferred_element_type=jnp.float32
                )
                * head_scale
            )
            shares = jnp.exp(logits - totals_img[:, offset : offset + block_rows, None])
            grad_shares = jnp.einsum(
                "qhe,khe->hqk", grad_block, values_img, preferred_element_type=jnp.float32
            )
            row_inner = jnp.sum(shares * grad_shares, axis=2, keepdims=True)
            grad_logits = (shares * (grad_shares - row_inner)).astype(jnp.bfloat16)
            query_parts.append(
                (
                    jnp.einsum(
                        "hqk,khe->qhe", grad_logits, keys_img, preferred_element_type=jnp.float32
                    )
                    * head_scale
                ).astype(jnp.bfloat16)
            )
            grad_keys_img = (
                grad_keys_img
                + jnp.einsum(
                    "hqk,qhe->khe", grad_logits, query_block, preferred_element_type=jnp.float32
                )
                * head_scale
            )
            grad_values_img = grad_values_img + jnp.einsum(
                "hqk,qhe->khe",
                shares.astype(jnp.bfloat16),
                grad_block,
                preferred_element_type=jnp.float32,
            )
        return (
            jnp.concatenate(query_parts, 0),
            grad_keys_img.astype(jnp.bfloat16),
            grad_values_img.astype(jnp.bfloat16),
        )

    grad_queries, grad_keys, grad_values = lax.map(
        attend_back,
        (
            by_head(queries),
            by_head(key_rows),
            by_head(value_rows),
            by_head(grad_attended),
            log_totals,
        ),
    )
    grad_queries = grad_queries.reshape(row_count, local_width)
    grad_keys = grad_keys.reshape(row_count, local_width)
    grad_values = grad_values.reshape(row_count, local_width)
    grad_query_bias = jnp.sum(grad_queries, axis=0, dtype=jnp.float32)
    grad_value_bias = jnp.sum(grad_values, axis=0, dtype=jnp.float32)
    grad_query_weight = inner_rows(flat_attn, grad_queries)
    grad_key_weight = inner_rows(flat_attn, grad_keys)
    grad_value_weight = inner_rows(flat_attn, grad_values)
    partial_normed = (
        against(grad_queries, back_query)
        + against(grad_keys, back_key)
        + against(grad_values, back_value)
    )
    grad_normed_attn = fold_grads(partial_normed.reshape(images, length, model_width))
    _, attn_pull = jax.vjp(modulate_images, inputs, shift_attn, scale_attn)
    grad_inputs, grad_shift_attn, grad_scale_attn = attn_pull(grad_normed_attn)
    grad_tokens = grad_after + grad_inputs
    modulation_terms = jnp.concatenate(
        [
            grad_shift_attn,
            grad_scale_attn,
            grad_gate_attn,
            grad_shift_mlp,
            grad_scale_mlp,
            grad_gate_mlp,
        ],
        axis=1,
    )
    grad_modulation = lax.psum_scatter(
        modulation_terms, "tensor", scatter_dimension=1, tiled=True
    ).astype(jnp.bfloat16)
    grad_ada_bias = jnp.sum(grad_modulation, axis=0, dtype=jnp.float32)
    grad_ada_weight = inner_rows(lifted_low, grad_modulation)
    grad_lifted = lax.psum(against(grad_modulation, back_ada), "tensor")
    _, silu_pull = jax.vjp(jax.nn.silu, conditioning)
    grad_conditioning = silu_pull(grad_lifted)[0]
    weight_grads = (
        lax.psum_scatter(grad_query_weight, "dp", scatter_dimension=0, tiled=True),
        lax.psum_scatter(grad_key_weight, "dp", scatter_dimension=0, tiled=True),
        lax.psum_scatter(grad_value_weight, "dp", scatter_dimension=0, tiled=True),
        lax.psum_scatter(grad_out_weight, "dp", scatter_dimension=1, tiled=True),
        lax.psum_scatter(grad_up_weight, "dp", scatter_dimension=0, tiled=True),
        lax.psum_scatter(grad_down_weight, "dp", scatter_dimension=1, tiled=True),
        lax.psum_scatter(grad_ada_weight, "dp", scatter_dimension=0, tiled=True),
    )
    bias_grads = lax.psum(
        (
            grad_query_bias,
            grad_value_bias,
            grad_out_bias,
            grad_up_bias,
            grad_down_bias,
            grad_ada_bias,
        ),
        "dp",
    )
    limit = threshold[0]
    factor = jnp.sqrt(limit / jnp.maximum(peaks, limit))
    column_factor = jnp.repeat(factor, HEAD_DIM)
    query_clipped = (query_weight.astype(jnp.float32) * column_factor).astype(jnp.bfloat16)
    key_clipped = (key_weight.astype(jnp.float32) * column_factor).astype(jnp.bfloat16)
    query_bias_clipped = query_bias * column_factor
    return (
        block_out,
        grad_tokens,
        grad_conditioning,
        weight_grads[0],
        weight_grads[1],
        weight_grads[2],
        weight_grads[3],
        weight_grads[4],
        weight_grads[5],
        weight_grads[6],
        bias_grads[0],
        bias_grads[1],
        bias_grads[2],
        bias_grads[3],
        bias_grads[4],
        bias_grads[5],
        query_clipped,
        key_clipped,
        query_bias_clipped,
    )


def one_image_per_chip(
    tokens, conditioning, cotangent, query_weight, key_weight, value_weight, out_weight, up_weight,
    down_weight, ada_weight, query_bias, value_bias, out_bias, up_bias, down_bias, ada_bias, threshold,
):
    y, x, c, z = (lax.axis_index(a) for a in AXES)
    batch = 4 * y + 2 * x + c
    first = jnp.concatenate([query_weight, key_weight, value_weight, out_weight.T], axis=1)
    shard = jnp.stack([first, up_weight, down_weight.T])
    lift_own = jnp.pad(jax.nn.silu(conditioning).astype(bf).astype(f32), ((0, 6), (0, 0)))
    z_bias = jnp.concatenate([query_bias, value_bias, up_bias])[None]
    (
        full, own_tokens, own_cotangent, lifted_rows, vectors, biases, normed_attn, qkv, mate_kv, attended, totals,
        peak, branch_attn, normed_mlp, active, slope, grad_down,
    ) = forward(shard, tokens, cotangent, lift_own, ada_weight, ada_bias[None], z_bias, out_bias[None])
    sums, block_rows, token_rows, _, _, _, grad_ada_weight, grad_ada_bias, lifted, totals = backward(
        full, own_tokens, own_cotangent, normed_attn, normed_mlp, qkv, mate_kv, attended, totals, peak, branch_attn,
        active, slope, grad_down, vectors, lifted_rows, ada_weight, down_bias[None],
    )
    own_lifted = lax.dynamic_slice(lifted.reshape(8, 16, ROWS), (0, 2 * batch, 0), (8, 2, ROWS))
    own_lifted = jnp.swapaxes(own_lifted, 0, 1).reshape(2, 8 * ROWS)
    _, silu_pull = jax.vjp(jax.nn.silu, conditioning)
    grad_conditioning = silu_pull(own_lifted)[0]
    first_bias = lax.dynamic_slice(totals, (z, 0), (1, COLS))[0]
    grad_query_bias = first_bias[:HS]
    grad_value_bias = first_bias[2 * HS : 3 * HS]
    grad_up_bias = lax.dynamic_slice(totals, (4 + z, 0), (1, COLS))[0]
    grad_out_bias = totals[8, :COLS]
    grad_down_bias = totals[9, :COLS]
    grad_ada_bias = grad_ada_bias[0]
    limit = threshold[0]
    peaks = lax.dynamic_slice(totals[:, COLS], (4 * z,), (4,))
    factor = jnp.sqrt(limit / jnp.maximum(peaks, limit))
    column_factor = jnp.repeat(factor, HEAD_DIM)
    query_clipped = (query_weight.astype(f32) * column_factor).astype(bf)
    key_clipped = (key_weight.astype(f32) * column_factor).astype(bf)
    return (
        block_rows,
        token_rows.astype(f32),
        grad_conditioning,
        sums[0, :, :HS],
        sums[0, :, HS : 2 * HS],
        sums[0, :, 2 * HS : 3 * HS],
        sums[0, :, 3 * HS :].T,
        sums[1],
        sums[2].T,
        grad_ada_weight,
        grad_query_bias,
        grad_value_bias,
        grad_out_bias,
        grad_up_bias,
        grad_down_bias,
        grad_ada_bias,
        query_clipped,
        key_clipped,
        query_bias * column_factor,
    )


def solution(mesh):
    if dict(mesh.shape) == {"dp": 8, "tensor": 4}:
        mesh = Mesh(mesh.devices.reshape(2, 2, 2, 4), AXES)
        split, heads, body = ("y", "x", "core"), "z", one_image_per_chip
    else:
        split, heads, body = "dp", "tensor", local
    weight, turned, bias = P(split, heads), P(heads, split), P(heads)
    rows = P(split, heads, None)
    in_specs = (
        rows, P(split, None), rows, weight, weight, weight, turned, weight, turned, weight,
        bias, bias, P(), bias, P(), bias, P(),
    )
    out_specs = (
        rows, rows, P(split, None), weight, weight, weight, turned, weight, turned, weight,
        bias, bias, P(), bias, P(), bias, weight, weight, bias,
    )
    return jax.shard_map(body, mesh=mesh, in_specs=in_specs, out_specs=out_specs, check_vma=False)
```

profile of v0, /device:TPU:28, one launch (start us, length us, event | category | flops | bytes accessed | tf_op | source)
XLA Modules:
  0.0 384.8 jit_solution(4942196277413970749)
XLA Ops:
  0.7 1.3 concatenate.6
  2.0 2.2 pad_maximum_fusion.shard
  4.2 0.6 pad_convert_fusion.lift_own
  4.9 0.1 concatenate.7
  4.9 0.6 broadcast_in_dim.16.z_bias
  5.5 0.0 copy-done.10
  5.5 0.6 broadcast_in_dim.15.ada_bias
  6.1 0.6 broadcast_in_dim.17.out_bias
  6.7 157.9 %forward.1 = (bf16[3,1152,4608]{2,1,0:T(8,128)(2,1)}, bf16[512,1152]{1,0:T(8,128)(2,1)}, bf16[512,1152]{1,0:T(8,128)(2,1)}, f32[16,144]{1,0:T(8,128)}, f32[8,115...) custom-call(bf16[3,144,1152]{2,1,0:T(8,128)(2,1)} %pad_maximum_fusio, ...), custom_call_target="tpu_custom_call" | custom-call | tf_op jit(solution)/shard_map/forward/pallas_call | solution.py:526
  164.7 0.6 broadcast_in_dim.18.down_bias
  165.3 203.7 %backward.1 = (f32[3,144,1152]{2,1,0:T(8,128)}, bf16[2,256,1152]{2,1,0:T(8,128)(2,1)}, bf16[2,256,1152]{2,1,0:T(8,128)(2,1)}, bf16[2,1152,4608]{2,1,0:T(8,128)(2...) custom-call(bf16[3,1152,4608]{2,1,0:T(8,128)(2,1)} %get-tuple-elemen, ...), custom_call_target="tpu_custom_call" | custom-call | tf_op jit(solution)/shard_map/backward/pallas_call | solution.py:1111
  369.0 0.0 copy-start
  369.0 3.0 convert_element_type.22
  372.0 0.0 copy-start.1
  372.0 1.1 slice_bitcast_fusion
  373.1 1.1 slice_bitcast_fusion.2
  374.2 0.8 slice.51
  375.7 0.1 sqrt_reduce_fusion
  375.8 0.1 broadcast_in_dim.19
  375.9 0.1 mul.60
  375.9 0.0 copy-done.3
  375.9 0.0 copy-done.4
  376.0 0.7 multiply_convert_fusion
  376.7 0.8 dynamic-slice_bitcast_fusion
  377.5 0.1 reshape.55
  377.6 0.6 fusion.1
  378.3 1.5 slice_reduce_fusion
  379.8 0.6 mul.64
  380.3 1.4 dynamic-slice_reduce_fusion.1
  381.7 0.6 reduce.5
  382.4 1.0 copy.41
  383.4 1.0 copy.42
  (23 shorter events, 0.1 us)
Async XLA Ops:
  0.7 3.5 copy-start.5
  0.7 4.2 %copy-start.6 = (f32[288]{0:T(512)S(1)}, f32[288]{0:T(512)}, u32[]{:S(2)}) copy-start(f32[288]{0:T(512)} %param.27) | copy-start | bytes 3460
  0.7 4.2 %copy-start.12 = (f32[288]{0:T(512)S(1)}, f32[288]{0:T(512)}, u32[]{:S(2)}) copy-start(f32[288]{0:T(512)} %param.28) | copy-start | bytes 3460
  0.7 4.2 %copy-start.7 = (f32[1152]{0:T(1024)S(1)}, f32[1152]{0:T(1024)}, u32[]{:S(2)}) copy-start(f32[1152]{0:T(1024)} %param.30) | copy-start | bytes 13828
  0.7 4.8 %copy-start.10 = (f32[1728]{0:T(1024)S(1)}, f32[1728]{0:T(1024)}, u32[]{:S(2)}) copy-start(f32[1728]{0:T(1024)} %param.32) | copy-start | bytes 20740
  0.7 5.4 %copy-start.8 = (f32[1152]{0:T(1024)S(1)}, f32[1152]{0:T(1024)}, u32[]{:S(2)}) copy-start(f32[1152]{0:T(1024)} %param.29) | copy-start | bytes 13828
  5.5 159.1 %copy-start.9 = (f32[1152]{0:T(1024)S(1)}, f32[1152]{0:T(1024)}, u32[]{:S(2)}) copy-start(f32[1152]{0:T(1024)} %param.31) | copy-start | bytes 13828
  369.0 3.0 copy-start
  372.0 4.0 %copy-start.3 = (bf16[144,288]{1,0:T(8,128)(2,1)S(1)}, bf16[144,288]{1,0:T(8,128)(2,1)}, u32[]{:S(2)}) copy-start(bf16[144,288]{1,0:T(8,128)(2,1)} %param.20) | copy-start | bytes 248836
  372.0 4.0 %copy-start.4 = (bf16[144,288]{1,0:T(8,128)(2,1)S(1)}, bf16[144,288]{1,0:T(8,128)(2,1)}, u32[]{:S(2)}) copy-start(bf16[144,288]{1,0:T(8,128)(2,1)} %param.21) | copy-start | bytes 248836
  372.0 9.8 %copy-start.11 = (f32[1,1728]{1,0:T(1,128)S(1)}, f32[1,1728]{1,0:T(1,128)}, u32[]{:S(2)}) copy-start(f32[1,1728]{1,0:T(1,128)} %get-tuple-element.64) | copy-start | bytes 20740
  372.0 10.4 %copy-start.1 = (bf16[2,256,1152]{2,1,0:T(8,128)(2,1)S(1)}, bf16[2,256,1152]{2,1,0:T(8,128)(2,1)}, u32[]{:S(2)}) copy-start(bf16[2,256,1152]{2,1,0:T(8,128)(2,1)} %get-tuple-element.97) | copy-start | bytes 3538948
  374.2 9.1 %copy-start.2 = (f32[144,1728]{1,0:T(8,128)S(1)}, f32[144,1728]{1,0:T(8,128)}, u32[]{:S(2)}) copy-start(f32[144,1728]{1,0:T(8,128)} %get-tuple-element.106) | copy-start | bytes 2985988
where the time goes:
time: 391 us; the launch traced here: 385 us
  Pallas kernels  362 us (93%)
  local copies, waits for them, and re-layouts  12.8 us (3%)
  other arithmetic  8.45 us (2%)
    pallas_call x1, Pallas kernels, backward(): pl.pallas_call(backward_kernel, name='backward', out_shape=(S((3,) + B, f...  204 us
    pallas_call x1, Pallas kernels, forward(): pl.pallas_call(forward_kernel, name='forward', out_shape=(S((3, 8 * ROWS,...  158 us

commit v1 on v0

--- a/solution.py
+++ b/solution.py
@@ -742,20 +742,20 @@
     ((Scatter.near, 1), (Scatter.line0, 1), (Scatter.fetch, 5)),
 )
 HEADS = (
-    ((Scatter.far, 4), (Scatter.core, 7), (Scatter.rows, 0)),
-    ((Scatter.bring, 5), (Scatter.rows, 1)),
-    ((Scatter.far, 5), (Scatter.rows, 2)),
-    ((Scatter.rows, 3),),
-    ((Scatter.near, 4), (Scatter.line0, 4), (Scatter.rows, 4)),
-    ((Scatter.bring, 6), (Scatter.far, 6), (Scatter.rows, 5)),
-    ((Scatter.begin, 8), (Scatter.near, 5), (Scatter.line0, 5), (Scatter.rows, 6)),
-    ((Scatter.bring, 7), (Scatter.far, 7), (Scatter.fetch, 8), (Scatter.line1, 0), (Scatter.line1, 1), (Scatter.rows, 7)),
-    ((Scatter.core, 8), (Scatter.line1, 2), (Scatter.line1, 3)),
-    ((Scatter.near, 6), (Scatter.line0, 6), (Scatter.line1, 4)),
-    ((Scatter.begin, 9), (Scatter.line2, 0), (Scatter.line2, 1)),
+    ((Scatter.bring, 4), (Scatter.near, 3), (Scatter.line0, 3), (Scatter.fetch, 7), (Scatter.rows, 0)),
+    ((Scatter.far, 4), (Scatter.core, 7), (Scatter.rows, 1)),
+    ((Scatter.bring, 5), (Scatter.rows, 2)),
+    ((Scatter.far, 5), (Scatter.rows, 3)),
+    ((Scatter.rows, 4),),
+    ((Scatter.near, 4), (Scatter.line0, 4), (Scatter.bring, 6), (Scatter.rows, 5)),
+    ((Scatter.begin, 8), (Scatter.far, 6), (Scatter.rows, 6)),
+    ((Scatter.near, 5), (Scatter.line0, 5), (Scatter.fetch, 8), (Scatter.line1, 0), (Scatter.line1, 1), (Scatter.rows, 7)),
+    ((Scatter.bring, 7), (Scatter.core, 8), (Scatter.far, 7), (Scatter.line1, 2), (Scatter.line1, 3)),
+    ((Scatter.line1, 4),),
+    ((Scatter.begin, 9), (Scatter.near, 6), (Scatter.line0, 6), (Scatter.line2, 0), (Scatter.line2, 1)),
     ((Scatter.fetch, 9), (Scatter.line2, 2), (Scatter.line2, 3), (Scatter.line1, 5)),
-    ((Scatter.core, 9), (Scatter.near, 7), (Scatter.line0, 7), (Scatter.line2, 4)),
-    ((Scatter.bring, 8), (Scatter.far, 8), (Scatter.line1, 6)),
+    ((Scatter.core, 9), (Scatter.near, 7), (Scatter.line0, 7)),
+    ((Scatter.bring, 8), (Scatter.far, 8), (Scatter.line1, 6), (Scatter.line2, 4)),
     ((Scatter.begin, 10), (Scatter.last, 0), (Scatter.last, 1), (Scatter.line2, 5)),
     ((Scatter.fetch, 10), (Scatter.last, 2), (Scatter.last, 3), (Scatter.line1, 7)),
 )
@@ -917,7 +917,6 @@
     flow.do((Scatter.core, 6),)
     load = fetch(x_in, cot, 0)
     gt[...] = gb[...].T
-    flow.do((Scatter.near, 3), (Scatter.line0, 3), (Scatter.fetch, 7), (Scatter.bring, 4))
     gn[...] = jnp.zeros_like(gn)
     load.wait()
     xt[...] = cot[...].T

time: 391 us -> 384 us (0.982)
  Pallas kernels: 362 us -> 354 us
    pallas_call x1, Pallas kernels: 204 us -> 196 us  [backward(): pl.pallas_call(backward_kernel, name='backward', out_shape=(S((3,) + B, f...]
where the time goes in v1:
time: 384 us; the launch traced here: 378 us
  Pallas kernels  354 us (92%)
  local copies, waits for them, and re-layouts  12.8 us (3%)
  other arithmetic  8.45 us (2%)
    pallas_call x1, Pallas kernels, backward(): pl.pallas_call(backward_kernel, name='backward', out_shape=(S((3,) + B, f...  196 us
    pallas_call x1, Pallas kernels, forward(): pl.pallas_call(forward_kernel, name='forward', out_shape=(S((3, 8 * ROWS,...  158 us

profile of v1, /device:TPU:28, one launch (start us, length us, event | category | flops | bytes accessed | tf_op | source)
XLA Modules:
  0.0 377.6 jit_solution(785231229735947433)
XLA Ops:
  0.7 0.0 copy-start.5
  0.7 0.0 copy-start.6
  0.7 1.3 concatenate.6
  2.0 2.2 pad_maximum_fusion.shard
  4.2 0.6 pad_convert_fusion.lift_own
  4.9 0.1 concatenate.7
  4.9 0.6 broadcast_in_dim.16.z_bias
  5.5 0.0 copy-done.10
  5.5 0.6 broadcast_in_dim.15.ada_bias
  6.1 0.6 broadcast_in_dim.17.out_bias
  6.7 157.9 %forward.1 = (bf16[3,1152,4608]{2,1,0:T(8,128)(2,1)}, bf16[512,1152]{1,0:T(8,128)(2,1)}, bf16[512,1152]{1,0:T(8,128)(2,1)}, f32[16,144]{1,0:T(8,128)}, f32[8,115...) custom-call(bf16[3,144,1152]{2,1,0:T(8,128)(2,1)} %pad_maximum_fusio, ...), custom_call_target="tpu_custom_call" | custom-call | tf_op jit(solution)/shard_map/forward/pallas_call | solution.py:526
  164.7 0.6 broadcast_in_dim.18.down_bias
  165.3 196.5 %backward.1 = (f32[3,144,1152]{2,1,0:T(8,128)}, bf16[2,256,1152]{2,1,0:T(8,128)(2,1)}, bf16[2,256,1152]{2,1,0:T(8,128)(2,1)}, bf16[2,1152,4608]{2,1,0:T(8,128)(2...) custom-call(bf16[3,1152,4608]{2,1,0:T(8,128)(2,1)} %get-tuple-elemen, ...), custom_call_target="tpu_custom_call" | custom-call | tf_op jit(solution)/shard_map/backward/pallas_call | solution.py:1110
  361.7 3.0 convert_element_type.22
  364.7 1.1 slice_bitcast_fusion
  365.9 1.1 slice_bitcast_fusion.2
  367.0 0.8 slice.51
  368.4 0.1 sqrt_reduce_fusion
  368.5 0.1 broadcast_in_dim.19
  368.6 0.1 mul.60
  368.7 0.0 copy-done.4
  368.7 0.7 multiply_convert_fusion
  369.4 0.8 dynamic-slice_bitcast_fusion
  370.3 0.1 reshape.55
  370.4 0.6 fusion.1
  371.0 1.5 slice_reduce_fusion
  372.5 0.6 mul.64
  373.1 1.4 dynamic-slice_reduce_fusion.1
  374.5 0.6 reduce.5
  375.1 1.0 copy.41
  376.1 0.0 copy-done.2
  376.1 1.0 copy.42
  (23 shorter events, 0.1 us)
Async XLA Ops:
  0.7 3.5 copy-start.5
  0.7 4.2 %copy-start.6 = (f32[288]{0:T(512)S(1)}, f32[288]{0:T(512)}, u32[]{:S(2)}) copy-start(f32[288]{0:T(512)} %param.27) | copy-start | bytes 3460
  0.7 4.2 %copy-start.12 = (f32[288]{0:T(512)S(1)}, f32[288]{0:T(512)}, u32[]{:S(2)}) copy-start(f32[288]{0:T(512)} %param.28) | copy-start | bytes 3460
  0.7 4.2 %copy-start.7 = (f32[1152]{0:T(1024)S(1)}, f32[1152]{0:T(1024)}, u32[]{:S(2)}) copy-start(f32[1152]{0:T(1024)} %param.30) | copy-start | bytes 13828
  0.7 4.8 %copy-start.10 = (f32[1728]{0:T(1024)S(1)}, f32[1728]{0:T(1024)}, u32[]{:S(2)}) copy-start(f32[1728]{0:T(1024)} %param.32) | copy-start | bytes 20740
  0.7 5.4 %copy-start.8 = (f32[1152]{0:T(1024)S(1)}, f32[1152]{0:T(1024)}, u32[]{:S(2)}) copy-start(f32[1152]{0:T(1024)} %param.29) | copy-start | bytes 13828
  5.5 159.1 %copy-start.9 = (f32[1152]{0:T(1024)S(1)}, f32[1152]{0:T(1024)}, u32[]{:S(2)}) copy-start(f32[1152]{0:T(1024)} %param.31) | copy-start | bytes 13828
  361.7 3.0 copy-start
  364.7 4.0 %copy-start.3 = (bf16[144,288]{1,0:T(8,128)(2,1)S(1)}, bf16[144,288]{1,0:T(8,128)(2,1)}, u32[]{:S(2)}) copy-start(bf16[144,288]{1,0:T(8,128)(2,1)} %param.20) | copy-start | bytes 248836
  364.7 4.0 %copy-start.4 = (bf16[144,288]{1,0:T(8,128)(2,1)S(1)}, bf16[144,288]{1,0:T(8,128)(2,1)}, u32[]{:S(2)}) copy-start(bf16[144,288]{1,0:T(8,128)(2,1)} %param.21) | copy-start | bytes 248836
  364.7 9.8 %copy-start.11 = (f32[1,1728]{1,0:T(1,128)S(1)}, f32[1,1728]{1,0:T(1,128)}, u32[]{:S(2)}) copy-start(f32[1,1728]{1,0:T(1,128)} %get-tuple-element.64) | copy-start | bytes 20740
  364.7 10.4 %copy-start.1 = (bf16[2,256,1152]{2,1,0:T(8,128)(2,1)S(1)}, bf16[2,256,1152]{2,1,0:T(8,128)(2,1)}, u32[]{:S(2)}) copy-start(bf16[2,256,1152]{2,1,0:T(8,128)(2,1)} %get-tuple-element.97) | copy-start | bytes 3538948
  367.0 9.1 %copy-start.2 = (f32[144,1728]{1,0:T(8,128)S(1)}, f32[144,1728]{1,0:T(8,128)}, u32[]{:S(2)}) copy-start(f32[144,1728]{1,0:T(8,128)} %get-tuple-element.106) | copy-start | bytes 2985988
